TPU v7x, 128 devices: a whole 4x4x4 slice. The times are simulated.
128 devices in a mesh: dp: 16 (over y_lo, x, core), tensor: 8 (over y_hi, z).
Axes of the slice: x: 4, y: 4 (y_hi: 2, y_lo: 2; y = y_hi * 2 + y_lo), z: 4, core: 2. Of those that a mesh axis runs over, the one named last changes fastest.
Arguments:
- tokens: bfloat16 [32768, 1536], P(('dp', 'tensor')), may hold values from -6 to 6
- norm_gain: float32 [1536], replicated, may hold values from 0.5 to 1.5
- w_gate: bfloat16 [1536, 3072], P('dp', 'tensor'), may hold values from -0.15625 to 0.15625
- w_inner: bfloat16 [1536, 3072], P('dp', 'tensor'), may hold values from -0.15625 to 0.15625
- w_bc: bfloat16 [1536, 256], P('dp'), may hold values from -0.15625 to 0.15625
- w_step: bfloat16 [1536, 48], P('dp', 'tensor'), may hold values from -0.15625 to 0.15625
- conv_inner: float32 [4, 3072], P(None, 'tensor'), may hold values from -3 to 3
- bias_inner: float32 [3072], P('tensor'), may hold values from -3 to 3
- conv_bc: float32 [4, 256], replicated, may hold values from -3 to 3
- bias_bc: float32 [256], replicated, may hold values from -3 to 3
- step_bias: float32 [48], P('tensor'), may hold values from -5 to -1
- decay_log: float32 [48], P('tensor'), may hold values from -2 to 2.5
- skip_gain: float32 [48], P('tensor'), may hold values from 0.5 to 1.5
- gate_gain: float32 [3072], P('tensor'), may hold values from 0.5 to 1.5
- w_out: bfloat16 [1536, 3072], P('dp', 'tensor'), may hold values from -0.109375 to 0.109375
- cotangent: bfloat16 [32768, 1536], P(('dp', 'tensor')), may hold values from -6 to 6
Outputs:
- output: bfloat16 [32768, 1536], P(('dp', 'tensor'))
- tokens_grad: float32 [32768, 1536], P(('dp', 'tensor'))
- norm_gain_grad: float32 [1536], replicated
- w_gate_grad: float32 [1536, 3072], P('dp', 'tensor')
- w_inner_grad: float32 [1536, 3072], P('dp', 'tensor')
- w_bc_grad: float32 [1536, 256], P('dp')
- w_step_grad: float32 [1536, 48], P('dp', 'tensor')
- conv_inner_grad: float32 [4, 3072], P(None, 'tensor')
- bias_inner_grad: float32 [3072], P('tensor')
- conv_bc_grad: float32 [4, 256], replicated
- bias_bc_grad: float32 [256], replicated
- step_bias_grad: float32 [48], P('tensor')
- decay_log_grad: float32 [48], P('tensor')
- skip_gain_grad: float32 [48], P('tensor')
- gate_gain_grad: float32 [3072], P('tensor')
- w_out_grad: float32 [1536, 3072], P('dp', 'tensor')
All inputs are finite; a program needn't handle non-finite values.
Results may differ from a plain program's by a relative error of at most 0.012.
Values may be sent and summed in bfloat16 or wider, within the bound.
A program may use at most 192 MiB of HBM per device.

v0:
```python
import jax
import jax.numpy as jnp
from jax import lax
from jax.experimental import pallas as pl
from jax.experimental.pallas import tpu as pltpu
from jax.sharding import Mesh
from jax.sharding import PartitionSpec as P

D = 1536
LEN = 1024
INNER = 3072
STATE = 128
BLOCK = 256
BLOCKS = LEN // BLOCK
GROUPS = 2
HEADS = 6
COLS = HEADS * 64
WIDE = GROUPS * COLS
STEPS = 2 * WIDE
PROJ = STEPS + GROUPS * 128
MORE = PROJ - WIDE
LOG2E = 1.4426950408889634
EPS = 1e-05
F32 = jnp.float32
BF16 = jnp.bfloat16
MESH = pl.DeviceIdType.MESH
AXES = ("yl", "x", "c", "yh", "z")
ANY = pl.BlockSpec(memory_space=pl.ANY)
VMEM = pl.BlockSpec(memory_space=pltpu.VMEM)
SHAPE = jax.ShapeDtypeStruct
ROOM = 60 * 2**20


def dot(a, b):
    return jnp.dot(a, b, preferred_element_type=F32)


def dot_nt(a, b):
    return lax.dot_general(a, b, (((1,), (1,)), ((), ())), preferred_element_type=F32)


def dot_tn(a, b):
    return lax.dot_general(a, b, (((0,), (0,)), ((), ())), preferred_element_type=F32)


def pieces(v, n):
    out = []
    for _ in range(n):
        hi = v.astype(BF16)
        out.append(hi)
        v = v - hi.astype(F32)
    return out


def dot_left(v, ones, n):
    return sum(dot(p, ones) for p in pieces(v, n))


def spread(v, ones):
    hi = v.astype(BF16).astype(F32)
    low = pltpu.roll(v - hi, 64, 1)
    return dot(jnp.where(iota(v.shape, 1) < 64, hi, low).astype(BF16), ones)


def folded(v, ones):
    hi = v.astype(BF16)
    low = (v - hi.astype(F32)).astype(BF16)
    return dot(hi, ones) + dot(low, ones)


def dot_right(ones, v, n):
    return sum(dot(ones, p) for p in pieces(v, n))


def iota(shape, axis):
    return lax.broadcasted_iota(jnp.int32, shape, axis)


def expander():
    row, col = iota((128, COLS), 0), iota((128, COLS), 1)
    return ((row & 63) == lax.shift_right_logical(col, 6)).astype(BF16)


def reducer():
    row, col = iota((COLS, 128), 0), iota((COLS, 128), 1)
    return (col == lax.shift_right_logical(row, 6)).astype(BF16)


def sigmoid(v):
    return 0.5 * jnp.tanh(0.5 * v) + 0.5


def lower(strict=False):
    row, col = iota((BLOCK, BLOCK), 0), iota((BLOCK, BLOCK), 1)
    return ((row > col) if strict else (row >= col)).astype(BF16)


def upper():
    return (iota((BLOCK, BLOCK), 0) <= iota((BLOCK, BLOCK), 1)).astype(BF16)


def token_row(v):
    v = sum(v[:, 128 * i : 128 * (i + 1)] for i in range(v.shape[1] // 128))
    ones = jnp.ones((8, 128), BF16)
    return sum(dot_nt(ones, p) for p in pieces(v, 3))[0:1, :]


class Net:
    def __init__(self, send, recv):
        self.send, self.recv, self.copies = send, recv, []
        self.at = {name: lax.axis_index(name) for name in AXES}
        self.at["y"] = self.at["yh"] * 2 + self.at["yl"]
        self.places = {(a, s): lax.rem(self.at[a] + s + 4, 4) for a in ("x", "y", "z") for s in (1, -1, 2)}
        self.other = 1 - self.at["c"]
        self.targets = {("c", 1): {"c": self.other}}
        for (a, s), place in self.places.items():
            self.targets[a, s] = {"yh": place // 2, "yl": lax.rem(place, 2)} if a == "y" else {a: place}

    def near(self, axis, step):
        return self.places[axis, step]

    def plan(self, src, dst, axis, step=1):
        copy = Copy(self, len(self.copies), src, dst, self.targets[axis, step])
        self.copies.append(copy)
        return copy

    def start(self, src, dst, axis, step=1):
        return self.plan(lambda: src, lambda: dst, axis, step).start()

    def around(self, src, dst, axis):
        return [self.start(src, dst, axis, step) for step in (1, -1, 2)]

    def greet(self, peers):
        here, self.peers = pltpu.get_barrier_semaphore(), len(peers)
        for peer in peers:
            pl.semaphore_signal(here, inc=1, device_id=self.targets[peer], device_id_type=MESH)

    def met(self):
        pl.semaphore_wait(pltpu.get_barrier_semaphore(), self.peers)

    def finish(self):
        for copy in self.copies:
            copy.arrived()
        for copy in self.copies:
            copy.left()


class Copy:
    def __init__(self, net, index, src, dst, target):
        self.net, self.index, self.src, self.dst, self.target = net, index, src, dst, target
        self.here, self.gone = False, False

    def made(self):
        return pltpu.make_async_remote_copy(
            src_ref=self.src(),
            dst_ref=self.dst(),
            send_sem=self.net.send.at[self.index],
            recv_sem=self.net.recv.at[self.index],
            device_id=self.target,
            device_id_type=MESH,
        )

    def start(self):
        self.made().start()
        return self

    def arrived(self):
        if not self.here:
            self.here = True
            self.made().wait_recv()

    def left(self):
        if not self.gone:
            self.gone = True
            self.made().wait_send()


def sems(n):
    return [pltpu.SemaphoreType.DMA((n,)), pltpu.SemaphoreType.DMA((n,))]


def rows(ref, first, count):
    return ref.at[pl.ds(pl.multiple_of(first, 16), count)]


def lanes(first, count):
    return pl.ds(pl.multiple_of(first, 128), count)


def arrive(copies):
    for copy in copies:
        copy.arrived()


HALVES = ((0, 1), (1, -1))


class GridSum:
    def __init__(self, net, first, held, spans, scratch, cut=(0, 96)):
        self.net, self.first, self.held, self.spans = net, first, held, spans
        self.land, self.mid, self.last = scratch
        self.rows = pl.ds(*cut)
        self.one, self.two = [], []
        for slot, step in enumerate((2, 1, -1)):
            if first == "x":
                self.plan(self.one, lambda step=step: held.at[:, net.near("x", step), self.rows], lambda slot=slot: self.land.at[slot], "x", step)
            else:
                self.plan(self.two, lambda step=step: self.mid.at[net.near("x", step)], lambda slot=slot: self.last.at[slot], "x", step)
            lane = 0
            for base, n in spans:
                there = lambda step=step, base=base, n=n: lanes(base + (net.near("y", step) // 2) * n, n)
                if first == "x":
                    src = lambda step=step, there=there: self.mid.at[lax.rem(net.near("y", step), 2), :, there()]
                    self.plan(self.two, src, lambda slot=slot, lane=lane, n=n: self.last.at[slot, :, pl.ds(lane, n)], "y", step)
                else:
                    src = lambda step=step, there=there: held.at[lax.rem(net.near("y", step), 2), :, self.rows, there()]
                    self.plan(self.one, src, lambda slot=slot, lane=lane, n=n: self.land.at[slot, :, :, pl.ds(lane, n)], "y", step)
                lane += n

    def plan(self, to, src, dst, axis, step):
        to.append(self.net.plan(src, dst, axis, step))

    def step1(self):
        for copy in self.one:
            copy.start()

    def step2(self):
        arrive(self.one)
        at = self.net.at
        if self.first == "x":
            self.mid[...] = self.total(self.held[:, at["x"], self.rows], self.land, slice(None)).astype(BF16)
        else:
            lane = 0
            for base, n in self.spans:
                cut = slice(lane, lane + n)
                own = self.held[at["yl"], :, self.rows, lanes(base + at["yh"] * n, n)]
                self.mid[:, :, cut] = self.total(own, self.land, cut).astype(BF16)
                lane += n
        for copy in self.two:
            copy.start()

    def total(self, own, others, cut):
        return (own.astype(F32) + others[0, ..., cut].astype(F32)) + (others[1, ..., cut].astype(F32) + others[2, ..., cut].astype(F32))

    def step3(self, out):
        arrive(self.two)
        at = self.net.at
        if self.first == "y":
            out[self.rows, :] = self.total(self.mid[at["x"]], self.last, slice(None))
            return
        lane = 0
        for base, n in self.spans:
            cut = slice(lane, lane + n)
            out[self.rows, cut] = self.total(self.mid[at["yl"], :, lanes(base + at["yh"] * n, n)], self.last, cut)
            lane += n


def grid_scratch(first, width, count=96):
    blocks, wide = (2, 2 * width) if first == "x" else (4, width)
    return [pltpu.VMEM(s, BF16) for s in ((3, blocks, count, wide), (blocks, count, wide), (3, count, width))]


class TokenSum:
    def __init__(self, net, scratch):
        self.net, self.far, self.half, self.fold, self.whole = net, *scratch
        self.one = [
            net.plan(lambda p=p: self.far.at[pl.ds(128 * p, 128)], lambda p=p: self.half.at[p], "z", step) for p, step in HALVES
        ]
        half = lambda ref, p, n: ref.at[p, pl.ds(128 * n, 128)]
        self.ready = [net.plan(lambda p=p: half(self.fold, p, 1 - p), lambda p=p: half(self.whole, p, 1 - p), "z", step) for p, step in HALVES]
        self.added = [net.plan(lambda p=p: half(self.fold, p, p), lambda p=p: half(self.whole, p, p), "z", step) for p, step in HALVES]

    def step1(self):
        for copy in self.one:
            copy.start()

    def folded(self, p):
        self.ready[p].start()

    def step2(self):
        arrive(self.one)
        for p, _ in HALVES:
            self.fold[p, 128 * p : 128 * p + 128, :] += self.half[p]
            self.added[p].start()

    def step3(self):
        arrive(self.ready + self.added)
        return self.whole[0].astype(F32) + self.whole[1].astype(F32)


def token_scratch():
    return [pltpu.VMEM((256, D), BF16), pltpu.VMEM((2, 128, D), BF16), pltpu.VMEM((2, 256, D), BF16), pltpu.VMEM((2, 256, D), BF16)]


def earlier(v, before, step):
    if step == 0:
        return v
    turned = pltpu.roll(v, step, 0)
    starts = jnp.where(iota(before.shape, 0) < step, pltpu.roll(before, step, 0), turned[0:8, :])
    return jnp.concatenate([starts, turned[8:, :]], axis=0)


def front_kernel(
    x, gain, w_gate, w_inner, w_out, w_bc, w_step, conv, bias, gate_gain, step_bias, decay_log, skip_gain, conv_bc, bias_bc, cot,
    inner_out, z_out, y_out, h_out, dt_out, r_out, bc_out, bcin_out, zbc_out, normed_t, gains_out,
    mixed_out, gs_out, gg_out, cot_t, normed_out, wx_out, wout_out, wbc_out, prm_out,
    normed, wx, wout, wbc, prm, xv, stepv, stept, pk,
    cots, gps, acts, slopes, gms, mixed, gg, turned_c, ext, extbc, state, stat, cross, slots, slots_c, send, recv, local,
):
    i = pl.program_id(0)
    net = Net(send, recv)
    at = net.at
    yh, cx, cc, z, y = at["yh"], at["x"], at["c"], at["z"], at["y"]
    own_rows = lambda ref: rows(ref, z * 256, 256)
    order = ((0, 1), (1, -1), (1, 1), (0, -1))
    part = lambda ref, p, s: rows(ref, net.near("z", -s) * 256 + 128 * p, 128)
    c1 = [
        net.plan(lambda p=p: cot.at[pl.ds(128 * p, 128)], lambda p=p: rows(cots, z * 256 + 128 * p, 128), "z", s) for p, s in order
    ]
    c2 = [net.plan(lambda p=p, s=s: part(cots, p, s), lambda p=p, s=s: part(cots, p, s), "z", s) for p, s in HALVES]
    q = [net.plan(lambda: stat, lambda: slots.at[z], "z", step) for step in (1, -1, 2)]
    qc = [net.plan(lambda: cross, lambda: slots_c.at[z], "z", step) for step in (1, -1, 2)]
    spot_o = lambda xx, cut=pl.ds(0, 96): wout.at[at["yl"], xx, cc, cut, lanes(yh * COLS, COLS)]
    line_o = lambda yy, cut=pl.ds(0, 96): wout.at[lax.rem(yy, 2), :, cc, cut, lanes((yy // 2) * COLS, COLS)]
    same = lambda ref, axis, step=1: net.plan(ref, ref, axis, step)
    o1 = [net.plan(lambda: w_out, lambda: spot_o(cx), "x", step) for _, step in HALVES]
    o2 = [same(lambda p=p, s=s: spot_o(net.near("x", -s), pl.ds(48 * p, 48)), "x", s) for p, s in HALVES]
    o3 = [same(lambda: line_o(y), "y", step) for _, step in HALVES]
    o4 = [same(lambda p=p, s=s: line_o(net.near("y", -s), pl.ds(48 * p, 48)), "y", s) for p, s in HALVES]
    oc = [same(lambda: line_o(y), "c")] + [same(lambda s=s: line_o(net.near("y", s)), "c") for s in (1, -1, 2)]
    own = lambda: pltpu.make_async_copy(cot, own_rows(cots), local.at[0])
    pairs = ((normed, normed_out), (wx, wx_out), (wbc, wbc_out), (prm, prm_out), (wout, wout_out))
    leave = lambda n: pltpu.make_async_copy(*pairs[n], local.at[1 + n])

    @pl.when(i == 0)
    def _():
        load = pltpu.make_async_copy(x, xv, local.at[7])
        load.start()
        net.greet([("z", 1), ("z", -1), ("z", 2), ("x", 1), ("x", -1), ("y", 1), ("y", -1), ("y", 2), ("c", 1)])
        own().start()
        stept[...] = jnp.zeros_like(stept)
        stept[0:HEADS, 0:96] = w_step[...].astype(F32)
        stepv[...] = jnp.transpose(stept[...])[0:96, :].astype(BF16)
        pk[...] = jnp.zeros_like(pk)
        pk[0:4, :] = conv[...]
        pk[4:5, :] = bias[...].reshape(1, COLS)
        pk[5:6, :] = gate_gain[...].reshape(1, COLS)
        pk[6:7, 0:HEADS] = step_bias[...].reshape(1, HEADS)
        pk[7:8, 0:HEADS] = decay_log[...].reshape(1, HEADS)
        pk[8:9, 0:HEADS] = skip_gain[...].reshape(1, HEADS)
        first = {
            "x": ((w_gate, wx, 0, COLS), (w_bc.at[:, lanes(yh * 128, 128)], wbc, 0, 128)),
            "y": ((w_inner, wx, WIDE, COLS), (stepv, wx, STEPS, 128)),
        }
        then = {"x": "y", "y": "x"}
        done = []

        def go(src, dst, axis, step=1):
            done.append(net.start(src, dst, axis, step))
            return done[-1]

        def spot(ref, base, n, yy, xx, cut=pl.ds(0, 96)):
            return ref.at[lax.rem(yy, 2), xx, cc, cut, lanes(base + (yy // 2) * n, n)]

        def line(axis, ref, base, n, place, cut=pl.ds(0, 96)):
            if axis == "x":
                return ref.at[lax.rem(place, 2), :, cc, cut, lanes(base + (place // 2) * n, n)]
            return ref.at[:, place, cc, cut, lanes(base, 2 * n)]

        load.wait()
        v = xv[...].astype(F32)
        root = lax.rsqrt(jnp.mean(v * v, axis=1, keepdims=True) + EPS)
        normed[pl.ds(pl.multiple_of(z * 256, 256), 256), :] = (v * root * gain[...].reshape(1, D)).astype(BF16)
        net.met()
        zs = {}
        for p, s in order:
            here = rows(normed, z * 256 + 128 * p, 128)
            zs[p, s] = go(here, here, "z", s)
        sent = {"x": [], "y": []}
        for axis in ("x", "y"):
            for src, ref, base, n in first[axis]:
                sent[axis].append([go(src, spot(ref, base, n, y, cx), axis, step) for _, step in HALVES])
        mine = [
            pltpu.make_async_copy(src, spot(ref, base, n, y, cx), local.at[8 + k])
            for k, (src, ref, base, n) in enumerate(first["x"] + first["y"])
        ]
        mine.append(pltpu.make_async_copy(pk, prm.at[yh], local.at[12]))
        mine.append(pltpu.make_async_copy(w_out, spot_o(cx), local.at[13]))
        for copy in mine:
            copy.start()
        for copy in o1:
            copy.start()
        for axis in ("x", "y"):
            for src, ref, base, n in first[axis]:
                go(src, spot(ref, base, n, y, cx), "c")
        go(pk, prm.at[yh], "y", 2)
        second = {"x": [], "y": []}
        for axis in ("x", "y"):
            for (src, ref, base, n), copies in zip(first[axis], sent[axis]):
                for (p, s), copy in zip(HALVES, copies):
                    copy.arrived()
                    cut = pl.ds(48 * p, 48)
                    here = spot(ref, base, n, y, net.near("x", -s), cut) if axis == "x" else spot(ref, base, n, net.near("y", -s), cx, cut)
                    second[axis].append(go(here, here, axis, s))
        for copy in mine:
            copy.wait()
        third = {"x": [], "y": []}
        for axis in ("x", "y"):
            arrive(second[axis])
            for src, ref, base, n in first[axis]:
                here = line(axis, ref, base, n, at[then[axis]])
                third[axis].append([go(here, here, then[axis], s) for _, s in HALVES])
        for copy, start in zip(o1, o2):
            copy.arrived()
            start.start()
        for axis in ("x", "y"):
            for src, ref, base, n in first[axis]:
                for s in (1, -1, 2):
                    here = spot(ref, base, n, y, net.near("x", s)) if axis == "x" else spot(ref, base, n, net.near("y", s), cx)
                    go(here, here, "c")
        for p, s in HALVES:
            zs[p, s].arrived()
            here = part(normed, p, s)
            go(here, here, "z", s)
        for copy in c1:
            copy.start()
        fourth = {"x": [], "y": []}
        for axis in ("x", "y"):
            for (src, ref, base, n), copies in zip(first[axis], third[axis]):
                for (p, s), copy in zip(HALVES, copies):
                    copy.arrived()
                    place = net.near(then[axis], -s)
                    here = line(axis, ref, base, n, place, pl.ds(48 * p, 48))
                    fourth[axis].append(go(here, here, then[axis], s))
                    here = line(axis, ref, base, n, place)
                    go(here, here, "c")
        arrive(o2)
        for copy in o3:
            copy.start()
        for axis in ("x", "y"):
            arrive(fourth[axis])
            for src, ref, base, n in first[axis]:
                here = line(axis, ref, base, n, net.near(then[axis], 2))
                go(here, here, "c")
        for copy in done:
            copy.arrived()
        for copy in done:
            copy.left()
        for n in range(4):
            leave(n).start()
        ext[...] = jnp.zeros_like(ext)
        extbc[...] = jnp.zeros_like(extbc)
        state[...] = jnp.zeros_like(state)
        stat[...] = jnp.zeros_like(stat)
        cross[...] = jnp.zeros_like(cross)

    @pl.when(i == 2)
    def _():
        for copy, start in zip(c1[:2], c2):
            copy.arrived()
            start.start()
        for copy, start in zip(o3, o4):
            copy.arrived()
            start.start()
        for copy in oc[:3]:
            copy.start()

    @pl.when(i < BLOCKS)
    def _():
        xb = normed[pl.ds(pl.multiple_of(i * BLOCK, BLOCK), BLOCK), :]
        turned = jnp.transpose(xb).reshape(2, 4, 2, 96, BLOCK)
        for core in range(2):
            normed_t[core] = turned[:, :, core]
        bc_in = dot(xb, wbc[...].reshape(D, 256))
        bcin_out[...] = bc_in.astype(BF16)
        before_bc = extbc[...]
        extbc[...] = bc_in[BLOCK - 8 :, :]
        zb = bias_bc[...].reshape(1, 256) + sum(conv_bc[j : j + 1, :] * earlier(bc_in, before_bc, 3 - j) for j in range(4))
        zbc_out[...] = zb.astype(BF16)
        bc = (zb * sigmoid(zb)).astype(BF16)
        bc_out[...] = bc
        b, c = bc[:, :STATE], bc[:, STATE:]
        scores = jnp.where(iota((BLOCK, BLOCK), 0) >= iota((BLOCK, BLOCK), 1), dot_nt(c, b), 0.0)
        tri, ones = lower(), expander()
        left = iota((BLOCK, 128), 1) < 64
        weight = lambda first, n: wx[:, :, :, :, first : first + n].reshape(D, n)
        steps = dot(xb, weight(STEPS, 256))
        total = jnp.zeros((BLOCK, 128), F32)
        for g in range(GROUPS):
            if g == 1:

                @pl.when(i == BLOCKS - 1)
                def _():
                    arrive(o4)
                    oc[3].start()

            cut = slice(g * COLS, (g + 1) * COLS)
            u = steps[:, 128 * g : 128 * (g + 1)] + prm[g, 6:7, 0:128]
            dt = jnp.maximum(u, 0.0) + jnp.log(1.0 + jnp.exp(-jnp.abs(u)))
            rate = -jnp.exp(prm[g, 7:8, 0:128]) * LOG2E
            r = dot_right(tri, dt * rate, 3)
            dt_out[g] = dt
            r_out[g] = r
            rt = jnp.transpose(r)
            gate = dot(xb, weight(g * COLS, COLS))
            inner = dot(xb, weight(WIDE + g * COLS, COLS))
            inner_out[:, cut] = inner.astype(BF16)
            before = ext[:, cut]
            ext[:, cut] = inner[BLOCK - 8 :, :]
            zv = prm[g, 4:5, :] + sum(prm[g, j : j + 1, :] * earlier(inner, before, 3 - j) for j in range(4))
            z_out[:, cut] = zv
            xv = zv * sigmoid(zv)
            last = r[BLOCK - 1 : BLOCK, :]
            w = xv * spread(dt, ones)
            grow = spread(jnp.exp2(r), ones)
            tail = spread(jnp.exp2(last - r), ones)
            skip = spread(prm[g, 8:16, 0:128], ones)[0:1, :]
            wl = w.astype(BF16)
            h = state[:, cut]
            h_out[0, g] = h.astype(BF16)
            parts = []
            for p in range(HEADS // 2):
                halves = []
                for n in (2 * p, 2 * p + 1):
                    gap = jnp.minimum(r[:, n : n + 1] - rt[n : n + 1, :], 0.0)
                    halves.append(dot((scores * jnp.exp2(gap)).astype(BF16), wl[:, 128 * p : 128 * (p + 1)]))
                parts.append(jnp.where(left, halves[0], halves[1]))
            yv = jnp.concatenate(parts, axis=1) + grow * dot(c, h.astype(BF16)) + skip * xv
            y_out[:, cut] = yv
            state[:, cut] = grow[BLOCK - 1 : BLOCK, :] * h + dot_tn(b, (tail * w).astype(BF16))
            sig = sigmoid(gate)
            act = gate * sig
            gp = yv * act
            here_now = pl.ds(pl.multiple_of(i * BLOCK, BLOCK), BLOCK)
            gps[here_now, cut] = gp
            acts[here_now, cut] = act
            slopes[here_now, cut] = yv * (sig + act * (1.0 - sig))
            sq = gp * gp
            total = total + (sq[:, 0:128] + sq[:, 128:256] + sq[:, 256:384])
        stat[pl.ds(i, 1), :] = token_row(total)

    @pl.when(i == BLOCKS)
    def _():
        for copy in q:
            copy.start()
        slots[z] = stat[...]
        own().wait()
        arrive(oc)
        leave(4).start()
        gain = jnp.concatenate([prm[0, 5:6, :], prm[1, 5:6, :]], axis=1)
        moved = []

        def away(src, dst, *cut):
            moved.append(pltpu.make_async_copy(src.at[cut], dst.at[cut], local.at[14 + len(moved)]))
            moved[-1].start()

        def place(n):
            block = lax.rem(z + n + lax.div(n, 2) - 2 * lax.div(n, 3), 4)
            return block, pl.ds(pl.multiple_of(block * BLOCK, BLOCK), BLOCK)

        def turn_out(n):
            full, (block, at) = slice(None), place(n)
            cut = (full, full, full, full, at)
            return pltpu.make_async_copy(turned_c.at[cut], cot_t.at[cut], local.at[26 + n])

        def products(n, nothing):
            @pl.when(n == 1)
            def _():
                arrive(c1)

            @pl.when(n == 3)
            def _():
                arrive(c2)

            block, at = place(n)
            cb = cots[at, :]
            turned = jnp.transpose(cb).reshape(2, 4, 2, 96, BLOCK)
            for core in range(2):
                turned_c[core, :, :, :, at] = turned[:, :, core]
            turn_out(n).start()
            gm = dot(cb, wout[...].reshape(D, WIDE)) * gain
            gms[at, :] = gm
            cross[pl.ds(block, 1), :] = token_row(gm * gps[at, :])
            return nothing

        lax.fori_loop(0, BLOCKS, products, 0)
        for copy in qc:
            copy.start()
        slots_c[z] = cross[...]
        arrive(q)
        for copy in q:
            copy.left()
        root = lax.rsqrt(((slots[0] + slots[1]) + (slots[2] + slots[3])) * (1.0 / INNER) + EPS)
        columns = jnp.transpose(root)
        gain_grad = jnp.zeros((1, WIDE), F32)
        for k in range(BLOCKS):
            at = slice(k * BLOCK, (k + 1) * BLOCK)
            normal, gm = gps[at, :] * columns[:, k : k + 1], gms[at, :]
            mixed[at, :] = (normal * gain).astype(BF16)
            away(mixed, mixed_out, pl.ds(k * BLOCK, BLOCK))
            gain_grad = gain_grad + jnp.sum(gm * normal, axis=0, keepdims=True)
            gms[at, :] = gm * columns[:, k : k + 1]
        gain_grad = gain_grad / gain
        arrive(qc)
        sums = (slots_c[0] + slots_c[1]) + (slots_c[2] + slots_c[3])
        columns = jnp.transpose(root * root * root * (sums * (1.0 / INNER)))
        for k in range(BLOCKS):
            at = slice(k * BLOCK, (k + 1) * BLOCK)
            gated = gms[at, :] - gps[at, :] * columns[:, k : k + 1]
            gms[at, :] = gated * acts[at, :]
            gg[at, :] = (gated * slopes[at, :]).astype(BF16)
            away(gms, gs_out, pl.ds(k * BLOCK, BLOCK))
            away(gg, gg_out, pl.ds(k * BLOCK, BLOCK))
        gains_out[...] = jnp.concatenate([gain_grad, jnp.zeros((7, WIDE), F32)], axis=0)
        for copy in c1 + c2 + qc + o1 + o2 + o3 + o4 + oc:
            copy.left()
        for copy in moved:
            copy.wait()
        for n in range(len(pairs)):
            leave(n).wait()
        for n in range(BLOCKS):
            turn_out(jnp.int32(n)).wait()


def run_front(*args):
    first = lambda k: jnp.minimum(k, BLOCKS - 1)
    keep = lambda *s: pl.BlockSpec(s, lambda k: (0,) * len(s))
    block = lambda n: pl.BlockSpec((BLOCK, n), lambda k: (first(k), 0))
    small = lambda: pl.BlockSpec((GROUPS, BLOCK, 128), lambda k: (0, first(k), 0))
    wide = SHAPE((LEN, WIDE), F32)
    narrow = SHAPE((GROUPS, LEN, 128), F32)
    bf = lambda *s: pltpu.VMEM(s, BF16)
    f32 = lambda *s: pltpu.VMEM(s, F32)
    return pl.pallas_call(
        front_kernel,
        grid=(BLOCKS + 1,),
        out_shape=[
            SHAPE((LEN, WIDE), BF16),
            wide,
            wide,
            SHAPE((BLOCKS, GROUPS, STATE, COLS), BF16),
            narrow,
            narrow,
            SHAPE((LEN, 256), BF16),
            SHAPE((LEN, 256), BF16),
            SHAPE((LEN, 256), BF16),
            SHAPE((2, 2, 4, 96, LEN), BF16),
            SHAPE((8, WIDE), F32),
            SHAPE((LEN, WIDE), BF16),
            wide,
            SHAPE((LEN, WIDE), BF16),
            SHAPE((2, 2, 4, 96, LEN), BF16),
            SHAPE((LEN, D), BF16),
            SHAPE((2, 4, 2, 96, PROJ), BF16),
            SHAPE((2, 4, 2, 96, WIDE), BF16),
            SHAPE((2, 4, 2, 96, 256), BF16),
            SHAPE((GROUPS, 16, COLS), F32),
        ],
        in_specs=[ANY, VMEM, ANY, ANY, ANY, ANY] + [VMEM] * 9 + [ANY],
        out_specs=[
            block(WIDE),
            block(WIDE),
            block(WIDE),
            pl.BlockSpec((1, GROUPS, STATE, COLS), lambda k: (first(k), 0, 0, 0)),
            small(),
            small(),
            block(256),
            block(256),
            block(256),
            pl.BlockSpec((2, 2, 4, 96, BLOCK), lambda k: (0, 0, 0, 0, first(k))),
            keep(8, WIDE),
        ]
        + [ANY] * 9,
        scratch_shapes=[
            bf(LEN, D),
            bf(2, 4, 2, 96, PROJ),
            bf(2, 4, 2, 96, WIDE),
            bf(2, 4, 2, 96, 256),
            f32(GROUPS, 16, COLS),
            bf(256, D),
            bf(96, 128),
            f32(128, 128),
            f32(16, COLS),
            bf(LEN, D),
            f32(LEN, WIDE),
            f32(LEN, WIDE),
            f32(LEN, WIDE),
            f32(LEN, WIDE),
            bf(LEN, WIDE),
            bf(LEN, WIDE),
            bf(2, 2, 4, 96, LEN),
            f32(8, WIDE),
            f32(8, 256),
            f32(STATE, WIDE),
            f32(8, BLOCK),
            f32(8, BLOCK),
            f32(4, 8, BLOCK),
            f32(4, 8, BLOCK),
        ]
        + sems(96)
        + [pltpu.SemaphoreType.DMA((30,))],
        compiler_params=pltpu.CompilerParams(collective_id=1, has_side_effects=True, vmem_limit_bytes=ROOM),
        name="front",
    )(*args)


def later(v, after, step):
    turned = pltpu.roll(v, BLOCK - step, 0)
    ends = jnp.where(iota(after.shape, 0) < 8 - step, turned[BLOCK - 8 :, :], pltpu.roll(after, 8 - step, 0))
    return jnp.concatenate([turned[: BLOCK - 8, :], ends], axis=0)


def backward_kernel(
    gs_in, inner, zin, y, hin, prm, bc, dt, r, gains, mixed, wout, cot_t, gg, normed_t, tokens, zbc, bc_in, conv_bc,
    cat_out, acc, acc_bc, branch_out, wout_out, wgate_out,
    ext, extbc, dstate, dst, dbc, held, got, away, mv, wv, cv, gv, nv, ownb, g0, g1, g2, g3, s1, s2, s3, t1, t2, t3, send, recv, local,
):
    k = pl.program_id(0)
    net = Net(send, recv)
    cc, z = net.at["c"], net.at["z"]
    cross = [net.plan(lambda n=n: away.at[n], lambda n=n: got.at[n], "c") for n in range(2)]
    token = TokenSum(net, (g0, g1, g2, g3))
    rings = (GridSum(net, "y", held.at[0], ((0, COLS),), (s1, s2, s3)), GridSum(net, "x", held.at[1], ((0, COLS),), (t1, t2, t3)))

    @pl.when(k == 0)
    def _():
        net.greet([("z", 1), ("z", -1)] + [(a, s) for a in ("x", "y") for s in (1, -1, 2)] + [("c", 1)])
        loads = [pltpu.make_async_copy(src, dst, local.at[n]) for n, (src, dst) in enumerate(((mixed, mv), (wout, wv), (cot_t, cv), (gg, gv), (normed_t, nv)))]
        for copy in loads:
            copy.start()
        loads[0].wait()
        loads[1].wait()
        branch = lambda place: dot_nt(mv[pl.ds(pl.multiple_of(place * 256, 256), 256), :], wv[...])
        grads = lambda left, right, core: dot(left[core].reshape(8 * 96, LEN), right[...]).astype(BF16).reshape(2, 4, 96, WIDE)
        g0[...] = branch(net.near("z", 2)).astype(BF16)
        net.met()
        token.step1()
        for p, step in HALVES:
            g2[p] = branch(net.near("z", step)).astype(BF16)
            token.folded(p)
        ownb[...] = branch(z)
        loads[2].wait()
        away[0] = grads(cv, mv, net.other)
        cross[0].start()
        loads[3].wait()
        loads[4].wait()
        away[1] = grads(nv, gv, net.other)
        cross[1].start()
        held[0] = grads(cv, mv, cc)
        held[1] = grads(nv, gv, cc)
        acc[...] = jnp.zeros_like(acc)
        acc_bc[...] = jnp.zeros_like(acc_bc)
        extbc[BLOCK : BLOCK + 8, :] = jnp.zeros((8, 256), F32)
        for g in range(GROUPS):
            acc[g, 5:6, :] = gains[0:1, g * COLS : (g + 1) * COLS]
        ext[BLOCK : BLOCK + 8, :] = jnp.zeros((8, WIDE), F32)
        dstate[...] = jnp.zeros_like(dstate)

    @pl.when(k > 0)
    def _():
        ext[BLOCK : BLOCK + 8, :] = ext[0:8, :]
        extbc[BLOCK : BLOCK + 8, :] = extbc[0:8, :]

    b, c = bc[:, :STATE], bc[:, STATE:]
    valid = iota((BLOCK, BLOCK), 1) >= iota((BLOCK, BLOCK), 0)
    scores = jnp.where(valid, dot_nt(b, c), 0.0)
    ones, fold = expander(), reducer()
    left = iota((BLOCK, 128), 1) < 64
    suffix, prefix = upper(), lower(strict=True)
    dst[...] = jnp.zeros_like(dst)
    dbc[...] = jnp.zeros_like(dbc)
    for g in range(GROUPS):
        if g == 0:

            @pl.when(k == 1)
            def _():
                token.step2()

            @pl.when(k == 3)
            def _():
                for ring in rings:
                    ring.step2()

        else:

            @pl.when(k == 0)
            def _():
                for n in range(2):
                    cross[n].arrived()
                    held[n] += got[n]
                    rings[n].step1()

        cut = slice(g * COLS, (g + 1) * COLS)
        yv = y[:, cut]
        gs = gs_in[:, cut]
        xi = inner[:, cut].astype(F32)
        zv = zin[:, cut]
        zs = sigmoid(zv)
        xv = zv * zs
        dtv = dt[g]
        rate = -jnp.exp(prm[g, 7:8, 0:128])
        rv = r[g]
        rt = jnp.transpose(rv)
        last = rv[BLOCK - 1 : BLOCK, :]
        dte = spread(dt[g], ones)
        grow = spread(jnp.exp2(rv), ones)
        tail = spread(jnp.exp2(last - rv), ones)
        skip = spread(prm[g, 8:16, 0:128], ones)[0:1, :]
        w = xv * dte
        wl = w.astype(BF16)
        gl = gs.astype(BF16)
        hl = hin[0, g]
        h = hl.astype(F32)
        dh = dstate[:, cut]
        dhl = dh.astype(BF16)
        parts = []
        for p in range(HEADS // 2):
            halves, shares = [], []
            pair = slice(128 * p, 128 * (p + 1))
            wp, gpair = wl[:, pair], gl[:, pair]
            zero = jnp.zeros_like(wp)
            w_low = pltpu.roll(w[:, pair] - wp.astype(F32), 64, 1).astype(BF16)
            g_low = (gs[:, pair] - gpair.astype(F32)).astype(BF16)
            g_turn = pltpu.roll(gpair.astype(F32), 64, 1).astype(BF16)
            for n in (2 * p, 2 * p + 1):
                decay = jnp.exp2(jnp.minimum(rt[n : n + 1, :] - rv[:, n : n + 1], 0.0))
                halves.append(dot((scores * decay).astype(BF16), gpair))
                pick = (lambda a, b: jnp.where(left, a, b)) if n % 2 == 0 else (lambda a, b: jnp.where(left, b, a))
                one = jnp.concatenate([pick(wp, w_low), pick(wp, zero)], axis=1)
                two = jnp.concatenate([pick(gpair, g_turn), g_low], axis=1)
                shares.append(dot_nt(one, two) * decay)
            parts.append(jnp.where(left, halves[0], halves[1]))
            dst[...] += shares[0] + shares[1]
        dwi = jnp.concatenate(parts, axis=1)
        dws = tail * dot(b, dhl)
        dw = dwi + dws
        skipgrad = gs * xv
        diff = folded(gl.astype(F32) * (yv - skip * xv) - wl.astype(F32) * dwi, fold)
        zsum = dot((w * dws).astype(BF16), fold)
        const = folded(jnp.sum(h * dh, axis=0, keepdims=True) * grow[BLOCK - 1 : BLOCK, :] + jnp.zeros((8, COLS), F32), fold)
        da = dot_right(suffix, diff, 3) + dot_right(prefix, zsum, 3) + const[0:1, :]
        dstep = (dot((xv * dw).astype(BF16), fold) + rate * da) * jnp.where(dtv < 0.02, dtv * (1.0 - dtv * (0.5 - dtv * (1.0 / 6.0))), 1.0 - jnp.exp(-dtv))
        cat_out[:, WIDE + 128 * g : WIDE + 128 * (g + 1)] = dstep.astype(BF16)
        gx = (grow * gs).astype(BF16)
        dbc[:, STATE:] += dot_nt(gx, hl)
        dbc[:, :STATE] += dot_nt((tail * w).astype(BF16), dhl)
        dstate[:, cut] = grow[BLOCK - 1 : BLOCK, :] * dh + dot_tn(c, gx)
        dx = dte * dw + skip * gs
        dz = dx * (zs * (1.0 + zv * (1.0 - zs)))
        after = ext[BLOCK : BLOCK + 8, cut]
        ext[0:8, cut] = dz[0:8, :]
        gi = jnp.zeros((BLOCK, COLS), F32)
        for j in range(4):
            moved = dz if j == 3 else later(dz, after, 3 - j)
            gi = gi + prm[g, j : j + 1, :] * moved
            acc[g, j : j + 1, :] += jnp.sum(xi * moved, axis=0, keepdims=True)
        cat_out[:, cut] = gi.astype(BF16)
        acc[g, 4:5, :] += jnp.sum(dz, axis=0, keepdims=True)
        acc[g, 6:7, 0:128] += jnp.sum(dstep, axis=0, keepdims=True)
        acc[g, 7:8, 0:128] += jnp.sum(da * dt[g], axis=0, keepdims=True) * rate
        acc[g, 8:9, 0:128] += folded(jnp.sum(skipgrad, axis=0, keepdims=True) + jnp.zeros((8, COLS), F32), fold)[0:1, :]
    ds = jnp.where(valid, dst[...], 0.0).astype(BF16)
    dbc[:, STATE:] += dot_tn(ds, b)
    dbc[:, :STATE] += dot(ds, c)
    zb = zbc[...].astype(F32)
    sig = sigmoid(zb)
    dz = dbc[...] * (sig + zb * sig * (1.0 - sig))
    extbc[0:BLOCK, :] = dz
    bi = bc_in[...].astype(F32)
    gi = jnp.zeros((BLOCK, 256), F32)
    for j in range(4):
        moved = extbc[3 - j : 3 - j + BLOCK, :]
        gi = gi + conv_bc[j : j + 1, :] * moved
        acc_bc[j : j + 1, :] += jnp.sum(bi * moved, axis=0, keepdims=True)
    acc_bc[4:5, :] += jnp.sum(dz, axis=0, keepdims=True)
    cat_out[:, MORE:] = gi.astype(BF16)

    @pl.when(k == BLOCKS - 1)
    def _():
        rings[0].step3(wout_out)
        rings[1].step3(wgate_out)
        branch_out[...] = (tokens[...].astype(F32) + (ownb[...] + token.step3())).astype(BF16)
        for copy in net.copies:
            copy.left()


def run_backward(*args):
    rev = lambda k: BLOCKS - 1 - k
    cols = lambda n: pl.BlockSpec((BLOCK, n), lambda k: (rev(k), 0))
    small = lambda: pl.BlockSpec((GROUPS, BLOCK, 128), lambda k: (0, rev(k), 0))
    keep = lambda *s: pl.BlockSpec(s, lambda k: (0,) * len(s))
    bf = lambda *s: pltpu.VMEM(s, BF16)
    f32 = lambda *s: pltpu.VMEM(s, F32)
    return pl.pallas_call(
        backward_kernel,
        grid=(BLOCKS,),
        out_shape=[
            SHAPE((LEN, MORE + 256), BF16),
            SHAPE((GROUPS, 16, COLS), F32),
            SHAPE((8, 256), F32),
            SHAPE((256, D), BF16),
            SHAPE((96, COLS), F32),
            SHAPE((96, COLS), F32),
        ],
        in_specs=[cols(WIDE)] * 4
        + [
            pl.BlockSpec((1, GROUPS, STATE, COLS), lambda k: (rev(k), 0, 0, 0)),
            keep(GROUPS, 16, COLS),
            cols(256),
            small(),
            small(),
            keep(8, WIDE),
        ]
        + [ANY] * 5
        + [keep(256, D), cols(256), cols(256), keep(4, 256)],
        out_specs=[cols(MORE + 256), keep(GROUPS, 16, COLS), keep(8, 256), keep(256, D), keep(96, COLS), keep(96, COLS)],
        scratch_shapes=[
            f32(BLOCK + 8, WIDE),
            f32(BLOCK + 8, 256),
            f32(STATE, WIDE),
            f32(BLOCK, BLOCK),
            f32(BLOCK, 256),
            bf(2, 2, 4, 96, WIDE),
            bf(2, 2, 4, 96, WIDE),
            bf(2, 2, 4, 96, WIDE),
            bf(LEN, WIDE),
            bf(D, WIDE),
            bf(2, 2, 4, 96, LEN),
            bf(LEN, WIDE),
            bf(2, 2, 4, 96, LEN),
            f32(256, D),
        ]
        + token_scratch()
        + grid_scratch("y", COLS)
        + grid_scratch("x", COLS)
        + sems(26)
        + [pltpu.SemaphoreType.DMA((5,))],
        compiler_params=pltpu.CompilerParams(collective_id=2, has_side_effects=True, vmem_limit_bytes=ROOM),
        name="backward",
    )(*args)


def tail_kernel(
    gg, cat, wx, normed_t, normed, acc, acc_bc, wbc, gain,
    tokens_out, inner_out, bc_out, small_out,
    far_gg, far_cat, ggv, catv, wxv, ntv, nv, wv, ownb, held, got, away, dbw, heldb, gotb, small, sp0, sp1, sp2, sp3, bz, by,
    g0, g1, g2, g3, a1, a2, a3, b1, b2, b3, c1, c2, c3, send, recv, local,
):
    net = Net(send, recv)
    at = net.at
    yh, cx, cc, z, y = at["yh"], at["x"], at["c"], at["z"], at["y"]
    net.greet([(a, s) for a in ("z", "x", "y") for s in (1, -1, 2)] + [("c", 1)])
    far_rows = lambda ref: rows(ref, net.near("z", 2) * 256, 256)
    pairs = ((far_rows(cat), far_cat), (far_rows(gg), far_gg), (wx, wxv), (wbc, wv), (cat, catv), (gg, ggv), (normed_t, ntv), (normed, nv))
    loads = [pltpu.make_async_copy(src, dst, local.at[i]) for i, (src, dst) in enumerate(pairs)]
    for copy in loads:
        copy.start()
    token = TokenSum(net, (g0, g1, g2, g3))
    spans = ((0, COLS), (WIDE, 128))
    rings = (GridSum(net, "x", held, spans, (a1, a2, a3), (0, 48)), GridSum(net, "y", held, spans, (b1, b2, b3), (48, 48)))
    ring_bc = GridSum(net, "x", heldb, ((0, 128),), (c1, c2, c3))

    def product(gates, others):
        return dot_nt(gates, wxv[:, 0:WIDE]) + dot_nt(others[:, 0:MORE], wxv[:, WIDE:]) + dot_nt(others[:, MORE:], wv[...])

    def block(place):
        cut = pl.ds(pl.multiple_of(place * 256, 256), 256)
        return product(ggv[cut, :], catv[cut, :])

    def of_norm(place, grad):
        cut = pl.ds(pl.multiple_of(place * 256, 256), 256)
        return jnp.sum(grad * nv[cut, :].astype(F32), axis=0, keepdims=True)

    for copy in loads[:4]:
        copy.wait()
    far = product(far_gg[...], far_cat[...])
    g0[...] = far.astype(BF16)
    net.met()
    token.step1()
    for copy in loads[4:7]:
        copy.wait()
    grads = lambda core, cut, n: dot(ntv[core].reshape(8 * 96, LEN), catv[:, cut]).astype(BF16).reshape(2, 4, 96, n)
    for core in range(2):
        dbw[core] = grads(core, slice(MORE, MORE + 256), 256)
    crossb = net.start(dbw.at[net.other], gotb, "c")
    loads[7].wait()
    norm_part = of_norm(net.near("z", 2), far)
    for p, step in HALVES:
        out = block(net.near("z", step))
        g2[p] = out.astype(BF16)
        norm_part = norm_part + of_norm(net.near("z", step), out)
        if p == 0:
            crossb.arrived()
            heldb[...] = dbw[cc] + gotb[...]
            ring_bc.step1()
    ownb[...] = block(z)
    norm_part = (norm_part + of_norm(z, ownb[...])) / gain[...].reshape(1, D)
    small[0:16, :] = acc[0]
    small[16:32, :] = acc[1]
    small[32:48, :] = jnp.zeros((16, COLS), F32)
    for k in range(4):
        small[32 + k : 33 + k, :] = norm_part[:, k * COLS : (k + 1) * COLS]
    small[36:41, 0:256] = acc_bc[0:5, :]
    sp0[z] = small[32:48, :]
    q = net.around(sp0.at[z], sp0.at[z], "z")
    for p, _ in HALVES:
        token.folded(p)
    ring_bc.step2()
    away[...] = grads(net.other, slice(0, MORE), MORE)
    cross = net.start(away, got, "c")
    held[...] = grads(cc, slice(0, MORE), MORE)
    cross.arrived()
    held[...] += got[...]
    ring_bc.step3(by.at[yh])
    qb = [net.start(by.at[yh], by.at[yh], "y", 2)]
    arrive(q)
    sp1[cx, 0:32, :] = small[0:32, :]
    sp1[cx, 32:48, :] = (sp0[0] + sp0[1]) + (sp0[2] + sp0[3])
    q = net.around(sp1.at[cx], sp1.at[cx], "x")
    for ring in rings:
        ring.step1()
    token.step2()
    arrive(qb)
    bz[z, :, 0:128] = by[0].astype(BF16)
    bz[z, :, 128:256] = by[1].astype(BF16)
    qb = net.around(bz.at[z], bz.at[z], "z")
    arrive(q)
    sp2[y] = (sp1[0] + sp1[1]) + (sp1[2] + sp1[3])
    q = net.around(sp2.at[y], sp2.at[y], "y")
    for ring in rings:
        ring.step2()
    arrive(q)
    sp3[cc] = (sp2[0] + sp2[1]) + (sp2[2] + sp2[3])
    q = [net.start(sp3.at[cc], sp3.at[cc], "c")]
    for ring in rings:
        ring.step3(inner_out)
    arrive(q)
    small_out[...] = sp3[0] + sp3[1]
    tokens_out[...] = token.step3() + ownb[...]
    arrive(qb)
    bc_out[...] = (bz[0].astype(F32) + bz[1].astype(F32)) + (bz[2].astype(F32) + bz[3].astype(F32))
    net.finish()


def run_tail(*args):
    bf = lambda *s: pltpu.VMEM(s, BF16)
    f32 = lambda *s: pltpu.VMEM(s, F32)
    return pl.pallas_call(
        tail_kernel,
        out_shape=[
            SHAPE((256, D), F32),
            SHAPE((96, COLS + 128), F32),
            SHAPE((96, 256), F32),
            SHAPE((48, COLS), F32),
        ],
        in_specs=[ANY] * 5 + [VMEM, VMEM, ANY, VMEM],
        out_specs=[VMEM] * 4,
        scratch_shapes=[
            bf(256, WIDE),
            bf(256, MORE + 256),
            bf(LEN, WIDE),
            bf(LEN, MORE + 256),
            bf(D, PROJ),
            bf(2, 2, 4, 96, LEN),
            bf(LEN, D),
            bf(D, 256),
            f32(256, D),
            bf(2, 4, 96, MORE),
            bf(2, 4, 96, MORE),
            bf(2, 4, 96, MORE),
            bf(2, 2, 4, 96, 256),
            bf(2, 4, 96, 256),
            bf(2, 4, 96, 256),
            f32(48, COLS),
            f32(4, 16, COLS),
            f32(4, 48, COLS),
            f32(4, 48, COLS),
            f32(2, 48, COLS),
            bf(4, 96, 256),
            f32(2, 96, 128),
        ]
        + token_scratch()
        + grid_scratch("x", COLS + 128, 48)
        + grid_scratch("y", COLS + 128, 48)
        + grid_scratch("x", 128)
        + sems(64)
        + [pltpu.SemaphoreType.DMA((8,))],
        compiler_params=pltpu.CompilerParams(collective_id=3, has_side_effects=True, vmem_limit_bytes=ROOM),
        name="tail",
    )(*args)


def finish_kernel(grad, tokens, cot, branch, norm_gain, inner, bc, small, gate, wout, tokens_out, branch_out, inner_out, bc_out, gate_out, wout_out, step_out, norm, conv, bias, conv_bc, bias_bc, step_bias, decay, skip, gain):
    v = tokens[...].astype(F32)
    root = lax.rsqrt(jnp.mean(v * v, axis=1, keepdims=True) + EPS)
    scaled = grad[...] * norm_gain[...].reshape(1, D)
    tokens_out[...] = cot[...].astype(F32) + root * scaled - v * (root * root * root) * jnp.mean(scaled * v, axis=1, keepdims=True)
    branch_out[...] = branch[...]

    @pl.when(pl.program_id(0) == 0)
    def _():
        inner_out[...] = inner[:, :COLS]
        bc_out[...] = bc[...]
        gate_out[...] = gate[...]
        wout_out[...] = wout[...]
        step_out[...] = jnp.transpose(jnp.concatenate([inner[:, COLS:], jnp.zeros((32, 128), F32)], axis=0))[0:HEADS, 0:96]
        norm[...] = jnp.concatenate([small[32 + k : 33 + k, :] for k in range(4)], axis=1).reshape(D)
        conv_bc[...] = small[36:40, 0:256]
        bias_bc[...] = small[40:41, 0:256].reshape(256)
        mine = small[pl.ds(pl.multiple_of(lax.axis_index("yh") * 16, 8), 16), :]
        conv[...] = mine[0:4, :]
        bias[...] = mine[4:5, :].reshape(COLS)
        gain[...] = mine[5:6, :].reshape(COLS)
        step_bias[...] = mine[6:7, 0:HEADS].reshape(HEADS)
        decay[...] = mine[7:8, 0:HEADS].reshape(HEADS)
        skip[...] = mine[8:9, 0:HEADS].reshape(HEADS)


def run_finish(*args):
    f32 = lambda *s: SHAPE(s, F32)
    strip = lambda: pl.BlockSpec((128, D), lambda k: (k, 0))
    whole = lambda *s: pl.BlockSpec(s, lambda k: (0,) * len(s))
    shapes = (
        (96, COLS), (96, 256), (96, COLS), (96, COLS), (HEADS, 96), (D,), (4, COLS), (COLS,), (4, 256), (256,), (HEADS,), (HEADS,), (HEADS,), (COLS,),
    )
    return pl.pallas_call(
        finish_kernel,
        grid=(2,),
        out_shape=[f32(256, D), SHAPE((256, D), BF16)] + [f32(*s) for s in shapes],
        in_specs=[strip(), strip(), strip(), strip()]
        + [whole(*s) for s in ((D,), (96, COLS + 128), (96, 256), (48, COLS), (96, COLS), (96, COLS))],
        out_specs=[strip(), strip()] + [whole(*s) for s in shapes],
        compiler_params=pltpu.CompilerParams(vmem_limit_bytes=ROOM),
        name="finish",
    )(*args)


def shards(tokens, norm_gain, w_gate, w_inner, w_bc, w_step, conv_inner, bias_inner, conv_bc, bias_bc, step_bias, decay_log, skip_gain, gate_gain, w_out, cotangent):
    (
        inner, zin, y, hin, dt, r, bc, bc_in, zbc, normed_t, gains, mixed, gs, gg, cot_t, normed, wx, wout, wbc, prm,
    ) = run_front(
        tokens, norm_gain, w_gate, w_inner, w_out, w_bc, w_step.T, conv_inner, bias_inner, gate_gain, step_bias, decay_log,
        skip_gain, conv_bc, bias_bc, cotangent,
    )
    wx, wout, wbc = wx.reshape(D, PROJ), wout.reshape(D, WIDE), wbc.reshape(D, 256)
    cat, acc, acc_bc, output, wout_grad, gate_grad = run_backward(
        gs, inner, zin, y, hin, prm, bc, dt, r, gains, mixed, wout, cot_t, gg, normed_t, tokens, zbc, bc_in, conv_bc
    )
    grad, inner_grad, bc_grad, small = run_tail(gg, cat, wx, normed_t, normed, acc, acc_bc, wbc, norm_gain)
    (
        tokens_grad, output, inner_grad, bc_grad, gate_grad, wout_grad, step_grad,
        norm, conv, bias, conv_bc_grad, bias_bc_grad, step_bias_grad, decay, skip, gate_gain_grad,
    ) = run_finish(grad, tokens, cotangent, output, norm_gain, inner_grad, bc_grad, small, gate_grad, wout_grad)
    return (
        output, tokens_grad, norm, gate_grad, inner_grad, bc_grad, step_grad.T, conv, bias, conv_bc_grad,
        bias_bc_grad, step_bias_grad, decay, skip, gate_gain_grad, wout_grad,
    )


def solution(mesh):
    fine = Mesh(mesh.devices.reshape(2, 4, 2, 2, 4), AXES)
    dp, tensor = ("yl", "x", "c"), ("yh", "z")
    tokens, weight = P(dp + tensor, None), P(dp, tensor)
    heads, shared = P(tensor), P()
    return jax.shard_map(
        shards,
        mesh=fine,
        in_specs=(
            tokens, shared, weight, weight, P(dp, None), weight, P(None, tensor), heads,
            shared, shared, heads, heads, heads, heads, weight, tokens,
        ),
        out_specs=(
            tokens, tokens, shared, weight, weight, P(dp, None), weight, P(None, tensor), heads,
            shared, shared, heads, heads, heads, heads, weight,
        ),
        check_vma=False,
    )
```

profile of v0, /device:TPU:0, one launch (start us, length us, event | category | flops | bytes accessed | tf_op | source)
XLA Modules:
  0.0 159.4 jit_solution(9886395215321541931)
XLA Ops:
  0.7 71.2 %front.1 = (bf16[1024,768]{1,0:T(8,128)(2,1)}, f32[1024,768]{1,0:T(8,128)}, f32[1024,768]{1,0:T(8,128)}, bf16[4,2,128,384]{3,2,1,0:T(8,128)(2,1)}, f32[2,1024,12...) custom-call(bf16[256,1536]{1,0:T(8,128)(2,1)} %tokens.3, ...), custom_call_target="tpu_custom_call" | custom-call | tf_op jit(solution)/shard_map/front/pallas_call | solution.py:634
  71.9 40.5 %backward.1 = (bf16[1024,1280]{1,0:T(8,128)(2,1)}, f32[2,16,384]{2,1,0:T(8,128)}, f32[8,256]{1,0:T(8,128)}, bf16[256,1536]{1,0:T(8,128)(2,1)}, f32[96,384]{1,0:T(8,128)}, /*index=5*/f32[96,384]{1,0:T(8,128)}) custom-call(f32[1024,768]{1,0:T(8,128)} %get-tuple-element.63.gs_in, bf16[1024,768]{1,0:T(8,128)(2,1)} %get-tuple-element.64.inner, ...), custom_call_target="tpu_custom_call" | custom-call | tf_op jit(solution)/shard_map/backward/pallas_call | solution.py:894
  112.4 42.9 %tail.1 = (f32[256,1536]{1,0:T(8,128)}, f32[96,512]{1,0:T(8,128)}, f32[96,256]{1,0:T(8,128)}, f32[48,384]{1,0:T(8,128)}) custom-call(bf16[1024,768]{1,0:T(8,128)(2,1)} %get-tuple-element.62.gg, bf16[1024,1280]{1,0:T(8,128)(2,1)} %get-tuple-element.79.cat, bf16[1536,1792]{1,0:T(8,128)(2,1)} %bitcast.5, ...), custom_call_target="tpu_custom_call" | custom-call | tf_op jit(solution)/shard_map/tail/pallas_call | solution.py:1048
  155.2 4.0 %finish.1 = (f32[256,1536]{1,0:T(8,128)}, bf16[256,1536]{1,0:T(8,128)(2,1)}, f32[96,384]{1,0:T(8,128)}, f32[96,256]{1,0:T(8,128)}, f32[96,384]{1,0:T(8,128)}, /*...) custom-call(f32[256,1536]{1,0:T(8,128)} %get-tuple-element.85.grad, ...), custom_call_target="tpu_custom_call" | custom-call | tf_op jit(solution)/shard_map/finish/pallas_call | solution.py:1126
where the time goes:
time: 160 us; the launch traced here: 159 us
  Pallas kernels  159 us (99%)
    pallas_call x1, Pallas kernels, run_front(): pl.pallas_call(front_kernel, grid=(BLOCKS + 1,), out_shape=[SHAPE((LEN, W...  71.2 us
    pallas_call x1, Pallas kernels, run_tail(): pl.pallas_call(tail_kernel, out_shape=[SHAPE((256, D), F32), SHAPE((96, C...  42.9 us
    pallas_call x1, Pallas kernels, run_backward(): pl.pallas_call(backward_kernel, grid=(BLOCKS,), out_shape=[SHAPE((LEN, MO...  40.5 us
    pallas_call x1, Pallas kernels, run_finish(): pl.pallas_call(finish_kernel, grid=(2,), out_shape=[f32(256, D), SHAPE((2...  3.96 us

commit v1 on v0

--- a/solution.py
+++ b/solution.py
@@ -496,7 +496,9 @@
 
             cut = slice(g * COLS, (g + 1) * COLS)
             u = steps[:, 128 * g : 128 * (g + 1)] + prm[g, 6:7, 0:128]
-            dt = jnp.maximum(u, 0.0) + jnp.log(1.0 + jnp.exp(-jnp.abs(u)))
+            low = jnp.exp(-jnp.abs(u))
+            series = low * (1.0 - low * (0.5 - low * (1.0 / 3.0 - low * 0.25)))
+            dt = jnp.maximum(u, 0.0) + jnp.where(low < 0.01, series, jnp.log(1.0 + low))
             rate = -jnp.exp(prm[g, 7:8, 0:128]) * LOG2E
             r = dot_right(tri, dt * rate, 3)
             dt_out[g] = dt

time: 160 us -> 161 us (level)
  no operation moved by 1% of the time
where the time goes in v1:
time: 161 us; the launch traced here: 160 us
  Pallas kernels  159 us (99%)
    pallas_call x1, Pallas kernels, run_front(): pl.pallas_call(front_kernel, grid=(BLOCKS + 1,), out_shape=[SHAPE((LEN, W...  71.5 us
    pallas_call x1, Pallas kernels, run_tail(): pl.pallas_call(tail_kernel, out_shape=[SHAPE((256, D), F32), SHAPE((96, C...  42.9 us
    pallas_call x1, Pallas kernels, run_backward(): pl.pallas_call(backward_kernel, grid=(BLOCKS,), out_shape=[SHAPE((LEN, MO...  40.5 us
    pallas_call x1, Pallas kernels, run_finish(): pl.pallas_call(finish_kernel, grid=(2,), out_shape=[f32(256, D), SHAPE((2...  3.96 us

profile of v1, /device:TPU:0, one launch (start us, length us, event | category | flops | bytes accessed | tf_op | source)
XLA Modules:
  0.0 159.7 jit_solution(7835655382590090192)
XLA Ops:
  0.7 71.5 %front.1 = (bf16[1024,768]{1,0:T(8,128)(2,1)}, f32[1024,768]{1,0:T(8,128)}, f32[1024,768]{1,0:T(8,128)}, bf16[4,2,128,384]{3,2,1,0:T(8,128)(2,1)}, f32[2,1024,12...) custom-call(bf16[256,1536]{1,0:T(8,128)(2,1)} %tokens.3, ...), custom_call_target="tpu_custom_call" | custom-call | tf_op jit(solution)/shard_map/front/pallas_call | solution.py:636
  72.2 40.5 %backward.1 = (bf16[1024,1280]{1,0:T(8,128)(2,1)}, f32[2,16,384]{2,1,0:T(8,128)}, f32[8,256]{1,0:T(8,128)}, bf16[256,1536]{1,0:T(8,128)(2,1)}, f32[96,384]{1,0:T(8,128)}, /*index=5*/f32[96,384]{1,0:T(8,128)}) custom-call(f32[1024,768]{1,0:T(8,128)} %get-tuple-element.63.gs_in, bf16[1024,768]{1,0:T(8,128)(2,1)} %get-tuple-element.64.inner, ...), custom_call_target="tpu_custom_call" | custom-call | tf_op jit(solution)/shard_map/backward/pallas_call | solution.py:896
  112.7 42.9 %tail.1 = (f32[256,1536]{1,0:T(8,128)}, f32[96,512]{1,0:T(8,128)}, f32[96,256]{1,0:T(8,128)}, f32[48,384]{1,0:T(8,128)}) custom-call(bf16[1024,768]{1,0:T(8,128)(2,1)} %get-tuple-element.62.gg, bf16[1024,1280]{1,0:T(8,128)(2,1)} %get-tuple-element.79.cat, bf16[1536,1792]{1,0:T(8,128)(2,1)} %bitcast.5, ...), custom_call_target="tpu_custom_call" | custom-call | tf_op jit(solution)/shard_map/tail/pallas_call | solution.py:1050
  155.5 4.0 %finish.1 = (f32[256,1536]{1,0:T(8,128)}, bf16[256,1536]{1,0:T(8,128)(2,1)}, f32[96,384]{1,0:T(8,128)}, f32[96,256]{1,0:T(8,128)}, f32[96,384]{1,0:T(8,128)}, /*...) custom-call(f32[256,1536]{1,0:T(8,128)} %get-tuple-element.85.grad, ...), custom_call_target="tpu_custom_call" | custom-call | tf_op jit(solution)/shard_map/finish/pallas_call | solution.py:1128

commit v2 on v1

--- a/solution.py
+++ b/solution.py
@@ -1014,7 +1014,8 @@
     cross.arrived()
     held[...] += got[...]
     ring_bc.step3(by.at[yh])
-    qb = [net.start(by.at[yh], by.at[yh], "y", 2)]
+    bz[z] = by[yh].astype(BF16)
+    qb = net.around(bz.at[z], bz.at[z], "z")
     arrive(q)
     sp1[cx, 0:32, :] = small[0:32, :]
     sp1[cx, 32:48, :] = (sp0[0] + sp0[1]) + (sp0[2] + sp0[3])
@@ -1022,15 +1023,14 @@
     for ring in rings:
         ring.step1()
     token.step2()
-    arrive(qb)
-    bz[z, :, 0:128] = by[0].astype(BF16)
-    bz[z, :, 128:256] = by[1].astype(BF16)
-    qb = net.around(bz.at[z], bz.at[z], "z")
     arrive(q)
     sp2[y] = (sp1[0] + sp1[1]) + (sp1[2] + sp1[3])
     q = net.around(sp2.at[y], sp2.at[y], "y")
     for ring in rings:
         ring.step2()
+    arrive(qb)
+    by[yh] = (bz[0].astype(F32) + bz[1].astype(F32)) + (bz[2].astype(F32) + bz[3].astype(F32))
+    qb = [net.start(by.at[yh], by.at[yh], "y", 2)]
     arrive(q)
     sp3[cc] = (sp2[0] + sp2[1]) + (sp2[2] + sp2[3])
     q = [net.start(sp3.at[cc], sp3.at[cc], "c")]
@@ -1040,7 +1040,8 @@
     small_out[...] = sp3[0] + sp3[1]
     tokens_out[...] = token.step3() + ownb[...]
     arrive(qb)
-    bc_out[...] = (bz[0].astype(F32) + bz[1].astype(F32)) + (bz[2].astype(F32) + bz[3].astype(F32))
+    bc_out[:, 0:128] = by[0]
+    bc_out[:, 128:256] = by[1]
     net.finish()
 
 
@@ -1078,7 +1079,7 @@
             f32(4, 48, COLS),
             f32(4, 48, COLS),
             f32(2, 48, COLS),
-            bf(4, 96, 256),
+            bf(4, 96, 128),
             f32(2, 96, 128),
         ]
         + token_scratch()

time: 161 us -> 161 us (level)
  no operation moved by 1% of the time
where the time goes in v2:
time: 161 us
  Pallas kernels  160 us (99%)
    pallas_call x1, Pallas kernels, run_front(): pl.pallas_call(front_kernel, grid=(BLOCKS + 1,), out_shape=[SHAPE((LEN, W...  71.5 us
    pallas_call x1, Pallas kernels, run_tail(): pl.pallas_call(tail_kernel, out_shape=[SHAPE((256, D), F32), SHAPE((96, C...  43.8 us
    pallas_call x1, Pallas kernels, run_backward(): pl.pallas_call(backward_kernel, grid=(BLOCKS,), out_shape=[SHAPE((LEN, MO...  40.5 us
    pallas_call x1, Pallas kernels, run_finish(): pl.pallas_call(finish_kernel, grid=(2,), out_shape=[f32(256, D), SHAPE((2...  3.96 us

profile of v2, /device:TPU:0, one launch (start us, length us, event | category | flops | bytes accessed | tf_op | source)
XLA Modules:
  0.0 160.6 jit_solution(9248618701889429454)
XLA Ops:
  0.7 71.5 %front.1 = (bf16[1024,768]{1,0:T(8,128)(2,1)}, f32[1024,768]{1,0:T(8,128)}, f32[1024,768]{1,0:T(8,128)}, bf16[4,2,128,384]{3,2,1,0:T(8,128)(2,1)}, f32[2,1024,12...) custom-call(bf16[256,1536]{1,0:T(8,128)(2,1)} %tokens.3, ...), custom_call_target="tpu_custom_call" | custom-call | tf_op jit(solution)/shard_map/front/pallas_call | solution.py:636
  72.2 40.5 %backward.1 = (bf16[1024,1280]{1,0:T(8,128)(2,1)}, f32[2,16,384]{2,1,0:T(8,128)}, f32[8,256]{1,0:T(8,128)}, bf16[256,1536]{1,0:T(8,128)(2,1)}, f32[96,384]{1,0:T(8,128)}, /*index=5*/f32[96,384]{1,0:T(8,128)}) custom-call(f32[1024,768]{1,0:T(8,128)} %get-tuple-element.63.gs_in, bf16[1024,768]{1,0:T(8,128)(2,1)} %get-tuple-element.64.inner, ...), custom_call_target="tpu_custom_call" | custom-call | tf_op jit(solution)/shard_map/backward/pallas_call | solution.py:896
  112.7 43.8 %tail.1 = (f32[256,1536]{1,0:T(8,128)}, f32[96,512]{1,0:T(8,128)}, f32[96,256]{1,0:T(8,128)}, f32[48,384]{1,0:T(8,128)}) custom-call(bf16[1024,768]{1,0:T(8,128)(2,1)} %get-tuple-element.62.gg, bf16[1024,1280]{1,0:T(8,128)(2,1)} %get-tuple-element.79.cat, bf16[1536,1792]{1,0:T(8,128)(2,1)} %bitcast.5, ...), custom_call_target="tpu_custom_call" | custom-call | tf_op jit(solution)/shard_map/tail/pallas_call | solution.py:1051
  156.5 4.0 %finish.1 = (f32[256,1536]{1,0:T(8,128)}, bf16[256,1536]{1,0:T(8,128)(2,1)}, f32[96,384]{1,0:T(8,128)}, f32[96,256]{1,0:T(8,128)}, f32[96,384]{1,0:T(8,128)}, /*...) custom-call(f32[256,1536]{1,0:T(8,128)} %get-tuple-element.85.grad, ...), custom_call_target="tpu_custom_call" | custom-call | tf_op jit(solution)/shard_map/finish/pallas_call | solution.py:1129
